TPU v7x, 32 devices: a whole 2x2x4 slice. The times are simulated.
32 devices in a mesh: ctx: 8 (over z, x), tp: 4 (over y, core).
Axes of the slice: x: 2, y: 2, z: 4, core: 2. Of those that a mesh axis runs over, the one named last changes fastest.
Arguments:
- query_heads: bfloat16 [2048, 4096], P('ctx', 'tp'), may hold values from -10 to 10
- key_heads: bfloat16 [2048, 1024], P('ctx'), may hold values from -6 to 6
- value_heads: bfloat16 [2048, 1024], P('ctx'), may hold values from -6 to 6
- grad_rows: bfloat16 [2048, 4096], P(('ctx', 'tp')), may hold values from -6 to 6
- doc_lengths: int32 [4], replicated, may hold values from 1 to 7, 16 in all
Outputs:
- attn_out: bfloat16 [2048, 4096], P(('ctx', 'tp'))
- d_query: bfloat16 [2048, 4096], P('ctx', 'tp')
- d_key: bfloat16 [2048, 1024], P(('ctx', 'tp'))
- d_value: bfloat16 [2048, 1024], P(('ctx', 'tp'))
Inputs may be any that keep to these rules, and one draw needn't show every extreme that they name: `doc_lengths`: lengths of the packed row's documents in blocks of 128 tokens, in order; they sum to 16 and one is exactly 7.
All inputs are finite; a program needn't handle non-finite values.
Results may differ from a plain program's by a relative error of at most 0.025.
Values may be sent and summed in bfloat16 or wider, within the bound.
A program may use at most 64 MiB of HBM per device.

v0:
```python
import math

import jax
import jax.numpy as jnp
from jax import lax
from jax.sharding import PartitionSpec as P

H = 32
KVH = 8
HD = 128
BLK = 128
WIN = 3


def passed_along(value, axis, steps):
    count = lax.axis_size(axis)
    first, last = (max(0, -steps), min(count, count - steps))
    return lax.ppermute(value, axis, [(source, source + steps) for source in range(first, last)])


def attend_block(queries, window, grad_local, allowed):
    tokens, groups, per_group, width = queries.shape
    key_span = window.shape[1]
    keys_win = window[0].reshape(key_span, groups, width)
    vals_win = window[1].reshape(key_span, groups, width)
    scaling = 1.0 / math.sqrt(width)
    scores = (
        jnp.einsum("tgqd,kgd->gqtk", queries, keys_win, preferred_element_type=jnp.float32)
        * scaling
    )
    scores = jnp.where(allowed, scores, -jnp.inf)
    row_max = jnp.max(scores, axis=-1, keepdims=True)
    log_norm = row_max + jnp.log(jnp.sum(jnp.exp(scores - row_max), axis=-1, keepdims=True))
    prob_full = jnp.exp(scores - log_norm)
    prob_half = prob_full.astype(jnp.bfloat16)
    output_half = jnp.einsum(
        "gqtk,kgd->tgqd", prob_half, vals_win, preferred_element_type=jnp.float32
    ).astype(jnp.bfloat16)
    delta = jnp.sum(grad_local.astype(jnp.float32) * output_half.astype(jnp.float32), axis=-1)
    d_prob = jnp.einsum("tgqd,kgd->gqtk", grad_local, vals_win, preferred_element_type=jnp.float32)
    d_score = (prob_full * (d_prob - jnp.transpose(delta, (1, 2, 0))[..., None])).astype(
        jnp.bfloat16
    )
    d_query_loc = (
        jnp.einsum("gqtk,kgd->tgqd", d_score, keys_win, preferred_element_type=jnp.float32)
        * scaling
    ).astype(jnp.bfloat16)
    d_key_win = (
        jnp.einsum("gqtk,tgqd->kgd", d_score, queries, preferred_element_type=jnp.float32) * scaling
    )
    d_val_win = jnp.einsum(
        "gqtk,tgqd->kgd", prob_half, grad_local, preferred_element_type=jnp.float32
    )
    terms = jnp.stack(
        [d_key_win.reshape(key_span, groups * width), d_val_win.reshape(key_span, groups * width)],
        0,
    )
    return (output_half, d_query_loc, terms)


def local(query_heads, key_heads, value_heads, grad_rows, doc_lengths):
    tokens = query_heads.shape[0]
    heads_dev = query_heads.shape[1] // HD
    per_kv = H // KVH
    groups = max(1, heads_dev // per_kv)
    sharing = max(1, per_kv // heads_dev)
    per_group = heads_dev // groups
    position = lax.axis_index("ctx")
    lane_index = lax.axis_index("tp")
    first_group = lane_index * heads_dev // per_kv
    own_keys = lax.dynamic_slice_in_dim(key_heads, first_group * HD, groups * HD, 1)
    own_vals = lax.dynamic_slice_in_dim(value_heads, first_group * HD, groups * HD, 1)
    own_pair = jnp.stack([own_keys, own_vals], 0)
    grad_local = lax.all_to_all(grad_rows, "tp", split_axis=1, concat_axis=0, tiled=True)
    window = own_pair
    reach_now = 1
    while reach_now < WIN + 1:
        window = jnp.concatenate([passed_along(window, "ctx", reach_now), window], 1)
        reach_now = reach_now * 2
    key_span = window.shape[1]
    blocks_per = tokens // BLK
    block_ids = (position - WIN) * blocks_per + jnp.arange(key_span // BLK, dtype=jnp.int32)
    doc_ends = jnp.cumsum(doc_lengths)
    block_doc = jnp.sum((doc_ends[None, :] <= block_ids[:, None]).astype(jnp.int32), axis=1)
    block_doc = jnp.where(block_ids >= 0, block_doc, -1)
    key_doc = jnp.repeat(block_doc, BLK)
    query_doc = key_doc[WIN * tokens :]
    places = jnp.arange(key_span, dtype=jnp.int32)
    query_places = places[WIN * tokens :]
    allowed = (query_doc[:, None] == key_doc[None, :]) & (places[None, :] <= query_places[:, None])
    queries = query_heads.reshape(tokens, groups, per_group, HD)
    grads_split = grad_local.reshape(tokens, groups, per_group, HD)
    output_half, d_query_loc, terms = attend_block(queries, window, grads_split, allowed)
    attn_out = lax.all_to_all(
        output_half.reshape(tokens, heads_dev * HD), "tp", split_axis=0, concat_axis=1, tiled=True
    )
    summed_terms = terms
    reach_now = (WIN + 1) // 2
    while reach_now >= 1:
        lower_part = summed_terms[:, : reach_now * tokens]
        upper_part = summed_terms[:, reach_now * tokens :]
        summed_terms = upper_part + passed_along(lower_part, "ctx", -reach_now)
        reach_now = reach_now // 2
    pieces = summed_terms.reshape(2, tokens, groups, HD)
    regrouped = lax.all_to_all(pieces, "tp", split_axis=1, concat_axis=2, tiled=True)
    row_count = regrouped.shape[1]
    pair_sum = jnp.sum(regrouped.reshape(2, row_count, KVH, sharing, HD), axis=3)
    grads_out = pair_sum.reshape(2, row_count, KVH * HD).astype(jnp.bfloat16)
    return (attn_out, d_query_loc.reshape(tokens, heads_dev * HD), grads_out[0], grads_out[1])


def solution(mesh):
    return jax.shard_map(
        local,
        mesh=mesh,
        in_specs=(P("ctx", "tp"), P("ctx", None), P("ctx", None), P(("ctx", "tp"), None), P()),
        out_specs=(
            P(("ctx", "tp"), None),
            P("ctx", "tp"),
            P(("ctx", "tp"), None),
            P(("ctx", "tp"), None),
        ),
        check_vma=False,
    )
```

profile of v0, /device:TPU:11, one launch (start us, length us, event | category | flops | bytes accessed | tf_op | source)
XLA Modules:
  0.0 103.6 jit_solution(1127845667485091264)
XLA Ops:
  0.6 1.9 %copy.119 = bf16[8,4,8,1024]{3,2,0,1:T(8,128)(2,1)} copy(bf16[8,4,8,1024]{3,2,1,0:T(8,128)(2,1)} %bitcast.105) | data formatting | bytes 1048576 | tf_op jit(solution)/shard_map/all_to_all | solution.py:74
  2.5 4.1 %all-to-all-start.1 = ((bf16[64,4,1024]{2,0,1:T(8,128)(2,1)}), bf16[64,4,1024]{2,0,1:T(8,128)(2,1)S(1)}, u32[]{:S(2)}, u32[]{:S(2)}) async-start(bf16[64,4,1024]{2,0,1:T(8,128)(2,1)} %bitcast.88), calls=%async_computation.1 | async-start | bytes 1048576 | tf_op jit(solution)/shard_map/all_to_all | solution.py:74
  7.6 3.2 %collective-permute-start = (bf16[2,256,256]{2,1,0:T(8,128)(2,1)S(1)}, bf16[2,256,256]{2,1,0:T(8,128)(2,1)S(1)}, u32[]{:S(2)}, u32[]{:S(2)}) collective-permute-start(bf16[2,256,256]{2,1,0:T(8,128)(2,1)S(1)} %pad_maximum_fusion.1), channel_id=1, source_target_pairs={{0,4},{4,8},{8,12},{12,16},{16,20},{20,24},{24,28},{1,5},{5,9},{9,... | collective-permute-start | bytes 786440 | tf_op jit(solution)/shard_map/ppermute | solution.py:18
  11.8 5.6 %collective-permute-done = bf16[2,256,256]{2,1,0:T(8,128)(2,1)S(1)} collective-permute-done((bf16[2,256,256]{2,1,0:T(8,128)(2,1)S(1)}, bf16[2,256,256]{2,1,0:T(8,128)(2,1)S(1)}, u32[]{:S(2)}, u32[]{:S(2)}) %collective-permute-start) | collective-permute-done | bytes 262176 | tf_op jit(solution)/shard_map/ppermute | solution.py:18
  17.4 3.2 %collective-permute-start.1 = (bf16[2,512,256]{2,1,0:T(8,128)(2,1)S(1)}, bf16[2,512,256]{2,1,0:T(8,128)(2,1)}, u32[]{:S(2)}, u32[]{:S(2)}) collective-permute-start(bf16[2,512,256]{2,1,0:T(8,128)(2,1)S(1)} %maximum_maximum_fusion.1), channel_id=1, source_target_pairs={{0,8},{4,12},{8,16},{12,20},{16,24},{20,28},{1,9},{5,13},{9,17},{1... | collective-permute-start | bytes 1572872 | tf_op jit(solution)/shard_map/ppermute | solution.py:18
  20.8 1.2 %copy.113 = bf16[256,1024]{0,1:T(8,128)(2,1)S(1)} copy(bf16[256,1024]{1,0:T(8,128)(2,1)} %param.5) | data formatting | bytes 1048576 | tf_op jit(solution)/shard_map/reshape | solution.py:91
  23.1 8.9 %collective-permute-done.1 = bf16[2,512,256]{2,1,0:T(8,128)(2,1)} collective-permute-done((bf16[2,512,256]{2,1,0:T(8,128)(2,1)S(1)}, bf16[2,512,256]{2,1,0:T(8,128)(2,1)}, u32[]{:S(2)}, u32[]{:S(2)}) %collective-permute-start.1) | collective-permute-done | bytes 524320 | tf_op jit(solution)/shard_map/ppermute | solution.py:18
  32.0 1.1 %maximum_maximum_fusion = bf16[2,1024,256]{2,1,0:T(8,128)(2,1)S(1)} fusion(bf16[1,256,256]{2,1,0:T(8,128)(2,1)S(1)} %get-tuple-element.32, bf16[1,256,256]{2,1,0:T(8,128)(2,1)S(1)} %get-tuple-element.33, bf16[2,256,256]{2,1,0:T(8,128)(2,1)S(1)} %collective-permute-done, bf16[2,512,256]{2,1,0:T(8,128)(2,1)} %collective-permute-done.1), kind=kLoop, calls=%fused_computation.19 | loop fusion | flops 4194304 | bytes 2097152 | tf_op jit(solution)/shard_map/concatenate | solution.py:78
  33.6 1.4 %fusion.3 = (f32[2,4,256]{2,1,0:T(4,128)S(1)}, f32[2,1024,256,4]{2,1,3,0:T(8,128)S(1)}) fusion(pred[256,1024]{0,1:T(8,128)(4,1)S(1)} %fusion.9, bf16[1024,2,128,1]{0,2,3,1:T(8,128)(2,1)S(1)} %bitcast.94, bf16[256,2,4,128]{0,3,2,1:T(8,128)(2,1)S(1)} %bitcast.96), kind=kOutput, calls=%fused_computation.7 | convolution fusion | flops 543160320 | bytes 9707520 | tf_op jit(solution)/shard_map/tgqd,kgd->gqtk/dot_general | solution.py:28
  35.1 1.7 %exponential_reduce_fusion = f32[2,4,256]{2,1,0:T(4,128)S(1)} fusion(f32[2,1024,256,4]{2,1,3,0:T(8,128)S(1)} %get-tuple-element.29, f32[2,4,256]{2,1,0:T(4,128)S(1)} %get-tuple-element.28, pred[256,1024]{0,1:T(8,128)(4,1)S(1)} %fusion.9), kind=kLoop, calls=%fused_computation.5 | loop fusion | flops 8386560 | bytes 8667136 | tf_op jit(solution)/shard_map/reduce_sum | solution.py:33
  36.8 2.3 %fusion.10 = f32[2,1024,128,1]{1,2,3,0:T(8,128)S(1)} fusion(bf16[256,2,4,128]{0,3,2,1:T(8,128)(2,1)S(1)} %copy.88, f32[2,1024,256,4]{2,1,3,0:T(8,128)S(1)} %get-tuple-element.29, f32[2,4,256]{2,1,0:T(4,128)S(1)} %bitcast.111, pred[256,1024]{0,1:T(8,128)(4,1)S(1)} %fusion.9), kind=kOutput, calls=%fused_computation.36 | convolution fusion | flops 545259520 | bytes 10231808 | tf_op jit(solution)/shard_map/gqtk,tgqd->kgd/dot_general | solution.py:51
  39.1 2.3 %multiply_reduce_fusion = (f32[256,2,4]{0,2,1:T(4,128)S(1)}, bf16[256,2,4,128]{0,3,2,1:T(8,128)(2,1)S(1)}) fusion(bf16[256,2,4,128]{0,3,2,1:T(8,128)(2,1)S(1)} %copy.88, bf16[1024,2,128,1]{0,2,3,1:T(8,128)(2,1)S(1)} %bitcast.107, f32[2,1024,256,4]{2,1,3,0:T(8,128)S(1)} %get-tuple-element.29, f32[2,4,256]{2,1,0:T(4,128)S(1)} %bitcast.112, ...), kind=kOutput, calls=%fused_computation.20 | convolution fusion | flops 546568192 | bytes 10240000 | tf_op jit(solution)/shard_map/gqtk,kgd->tgqd/dot_general | solution.py:36
  41.4 2.7 %fusion.1 = bf16[2,4,256,1024]{2,3,1,0:T(8,128)(2,1)S(1)} fusion(f32[2,1024,256,4]{2,1,3,0:T(8,128)S(1)} %get-tuple-element.29, f32[2,4,256]{2,1,0:T(4,128)S(1)} %bitcast.116, f32[2,4,256]{2,1,0:T(4,128)S(1)} %bitcast.113, pred[256,1024]{0,1:T(8,128)(4,1)S(1)} %fusion.9, bf16[1024,2,128,1]{0,2,3,1:T(8,128)(2,1)S(1)} %bitcast.108, ...), kind=kOutput, calls=%fused_computation.2 | convolution fusion | flops 549453824 | bytes 13910016 | tf_op jit(solution)/shard_map/tgqd,kgd->gqtk/dot_general | solution.py:40
  44.1 1.9 %copy-done = bf16[2,4,256,1024]{2,3,1,0:T(8,128)(2,1)} copy-done((bf16[2,4,256,1024]{2,3,1,0:T(8,128)(2,1)}, bf16[2,4,256,1024]{2,3,1,0:T(8,128)(2,1)S(1)}, u32[]{:S(2)}) %copy-start) | copy-done | bytes 4194328
  46.0 1.5 %fusion.4 = f32[2,1024,128]{1,2,0:T(8,128)S(1)} fusion(bf16[2,4,256,1024]{2,3,1,0:T(8,128)(2,1)S(1)} %fusion.1, bf16[256,2,4,128]{0,3,2,1:T(8,128)(2,1)S(1)} %bitcast.97), kind=kOutput, calls=%fused_computation.11 | convolution fusion | flops 537133056 | bytes 5767168 | tf_op jit(solution)/shard_map/gqtk,tgqd->kgd/dot_general | solution.py:49
  47.6 2.1 %collective-permute-start.2 = (f32[2,512,256]{1,2,0:T(8,128)S(1)}, f32[2,512,256]{1,2,0:T(8,128)S(1)}, u32[]{:S(2)}, u32[]{:S(2)}) collective-permute-start(f32[2,512,256]{1,2,0:T(8,128)S(1)} %pad_maximum_fusion), channel_id=1, source_target_pairs={{8,0},{12,4},{16,8},{20,12},{24,16},{28,20},{9,1},{13,5},{17,9},{2... | collective-permute-start | bytes 3145736 | tf_op jit(solution)/shard_map/ppermute | solution.py:18
  49.7 22.7 %collective-permute-done.2 = f32[2,512,256]{1,2,0:T(8,128)S(1)} collective-permute-done((f32[2,512,256]{1,2,0:T(8,128)S(1)}, f32[2,512,256]{1,2,0:T(8,128)S(1)}, u32[]{:S(2)}, u32[]{:S(2)}) %collective-permute-start.2) | collective-permute-done | bytes 1048608 | tf_op jit(solution)/shard_map/ppermute | solution.py:18
  73.5 3.0 %collective-permute-start.3 = (f32[2,256,256]{1,2,0:T(8,128)}, f32[2,256,256]{1,2,0:T(8,128)S(1)}, u32[]{:S(2)}, u32[]{:S(2)}) collective-permute-start(f32[2,256,256]{1,2,0:T(8,128)} %slice.49), channel_id=1, source_target_pairs={{4,0},{8,4},{12,8},{16,12},{20,16},{24,20},{28,24},{5,1},{9,5},{13... | collective-permute-start | bytes 1572872 | tf_op jit(solution)/shard_map/ppermute | solution.py:18
  76.8 1.2 %all_to_all.33 = bf16[4,64,1024]{2,1,0:T(8,128)(2,1)} reshape(bf16[256,2,4,128]{3,2,1,0:T(4,128)(2,1)S(1)} %copy.83) | data formatting | bytes 1048576 | tf_op jit(solution)/shard_map/all_to_all | solution.py:94
  78.0 6.4 %all-to-all-start = ((bf16[4,64,1024]{2,1,0:T(8,128)(2,1)}), bf16[4,64,1024]{2,1,0:T(8,128)(2,1)S(1)}, u32[]{:S(2)}, u32[]{:S(2)}) async-start(bf16[4,64,1024]{2,1,0:T(8,128)(2,1)} %all_to_all.33), calls=%async_computation | async-start | bytes 1048576 | tf_op jit(solution)/shard_map/all_to_all | solution.py:94
  84.4 2.8 %collective-permute-done.3 = f32[2,256,256]{1,2,0:T(8,128)S(1)} collective-permute-done((f32[2,256,256]{1,2,0:T(8,128)}, f32[2,256,256]{1,2,0:T(8,128)S(1)}, u32[]{:S(2)}, u32[]{:S(2)}) %collective-permute-start.3) | collective-permute-done | bytes 524320 | tf_op jit(solution)/shard_map/ppermute | solution.py:18
  88.2 4.2 %all-to-all-done = bf16[4,64,1024]{2,1,0:T(8,128)(2,1)S(1)} async-done(((bf16[4,64,1024]{2,1,0:T(8,128)(2,1)}), bf16[4,64,1024]{2,1,0:T(8,128)(2,1)S(1)}, u32[]{:S(2)}, u32[]{:S(2)}) %all-to-all-start) | async-done | bytes 524320 | tf_op jit(solution)/shard_map/all_to_all | solution.py:94
  92.4 4.2 %all-to-all-start.2 = ((bf16[2,256,2,128]{3,2,0,1:T(2,128)(2,1)}), bf16[2,256,2,128]{3,2,0,1:T(2,128)(2,1)S(1)}, u32[]{:S(2)}, u32[]{:S(2)}) async-start(bf16[2,256,2,128]{3,2,0,1:T(2,128)(2,1)} %copy.94), calls=%async_computation.2 | async-start | bytes 524288 | tf_op jit(solution)/shard_map/all_to_all | solution.py:105
  96.6 2.9 %fusion.5 = bf16[2,128,4,256]{3,1,2,0:T(8,128)(2,1)S(1)} fusion(bf16[1024,2,128,1]{0,2,3,1:T(8,128)(2,1)S(1)} %bitcast.95, bf16[2,4,256,1024]{2,3,1,0:T(8,128)(2,1)} %copy-done), kind=kOutput, calls=%fused_computation.14 | convolution fusion | flops 537395200 | bytes 5242880 | tf_op jit(solution)/shard_map/gqtk,kgd->tgqd/dot_general | solution.py:45
  (36 shorter events, 10.1 us)
Async XLA Ops:
  2.5 19.9 %all-to-all-start.1 = ((bf16[64,4,1024]{2,0,1:T(8,128)(2,1)}), bf16[64,4,1024]{2,0,1:T(8,128)(2,1)S(1)}, u32[]{:S(2)}, u32[]{:S(2)}) async-start(bf16[64,4,1024]{2,0,1:T(8,128)(2,1)} %bitcast.88), calls=%async_computation.1 | async-start | bytes 1048576 | tf_op jit(solution)/shard_map/all_to_all | solution.py:74
  7.6 9.8 %collective-permute-start = (bf16[2,256,256]{2,1,0:T(8,128)(2,1)S(1)}, bf16[2,256,256]{2,1,0:T(8,128)(2,1)S(1)}, u32[]{:S(2)}, u32[]{:S(2)}) collective-permute-start(bf16[2,256,256]{2,1,0:T(8,128)(2,1)S(1)} %pad_maximum_fusion.1), channel_id=1, source_target_pairs={{0,4},{4,8},{8,12},{12,16},{16,20},{20,24},{24,28},{1,5},{5,9},{9,... | collective-permute-start | bytes 786440 | tf_op jit(solution)/shard_map/ppermute | solution.py:18
  17.4 14.6 %collective-permute-start.1 = (bf16[2,512,256]{2,1,0:T(8,128)(2,1)S(1)}, bf16[2,512,256]{2,1,0:T(8,128)(2,1)}, u32[]{:S(2)}, u32[]{:S(2)}) collective-permute-start(bf16[2,512,256]{2,1,0:T(8,128)(2,1)S(1)} %maximum_maximum_fusion.1), channel_id=1, source_target_pairs={{0,8},{4,12},{8,16},{12,20},{16,24},{20,28},{1,9},{5,13},{9,17},{1... | collective-permute-start | bytes 1572872 | tf_op jit(solution)/shard_map/ppermute | solution.py:18
  44.1 1.9 %copy-start = (bf16[2,4,256,1024]{2,3,1,0:T(8,128)(2,1)}, bf16[2,4,256,1024]{2,3,1,0:T(8,128)(2,1)S(1)}, u32[]{:S(2)}) copy-start(bf16[2,4,256,1024]{2,3,1,0:T(8,128)(2,1)S(1)} %fusion.1) | copy-start | bytes 12582916
  47.6 24.8 %collective-permute-start.2 = (f32[2,512,256]{1,2,0:T(8,128)S(1)}, f32[2,512,256]{1,2,0:T(8,128)S(1)}, u32[]{:S(2)}, u32[]{:S(2)}) collective-permute-start(f32[2,512,256]{1,2,0:T(8,128)S(1)} %pad_maximum_fusion), channel_id=1, source_target_pairs={{8,0},{12,4},{16,8},{20,12},{24,16},{28,20},{9,1},{13,5},{17,9},{2... | collective-permute-start | bytes 3145736 | tf_op jit(solution)/shard_map/ppermute | solution.py:18
  73.5 13.7 %collective-permute-start.3 = (f32[2,256,256]{1,2,0:T(8,128)}, f32[2,256,256]{1,2,0:T(8,128)S(1)}, u32[]{:S(2)}, u32[]{:S(2)}) collective-permute-start(f32[2,256,256]{1,2,0:T(8,128)} %slice.49), channel_id=1, source_target_pairs={{4,0},{8,4},{12,8},{16,12},{20,16},{24,20},{28,24},{5,1},{9,5},{13... | collective-permute-start | bytes 1572872 | tf_op jit(solution)/shard_map/ppermute | solution.py:18
  78.0 14.4 %all-to-all-start = ((bf16[4,64,1024]{2,1,0:T(8,128)(2,1)}), bf16[4,64,1024]{2,1,0:T(8,128)(2,1)S(1)}, u32[]{:S(2)}, u32[]{:S(2)}) async-start(bf16[4,64,1024]{2,1,0:T(8,128)(2,1)} %all_to_all.33), calls=%async_computation | async-start | bytes 1048576 | tf_op jit(solution)/shard_map/all_to_all | solution.py:94
  92.4 9.4 %all-to-all-start.2 = ((bf16[2,256,2,128]{3,2,0,1:T(2,128)(2,1)}), bf16[2,256,2,128]{3,2,0,1:T(2,128)(2,1)S(1)}, u32[]{:S(2)}, u32[]{:S(2)}) async-start(bf16[2,256,2,128]{3,2,0,1:T(2,128)(2,1)} %copy.94), calls=%async_computation.2 | async-start | bytes 524288 | tf_op jit(solution)/shard_map/all_to_all | solution.py:105
where the time goes:
time: 105 us; the launch traced here: 104 us
  waiting for transfers between devices  44.7 us (43%)
  starting transfers between devices  26.3 us (25%)
  local copies, waits for them, and re-layouts  14.2 us (14%)
  matrix products  13.1 us (12%)
  other arithmetic  4.47 us (4%)
    ppermute x4, waiting for transfers between devices, passed_along(): lax.ppermute(value, axis, [(source, source + steps) for source in range(f...  40 us
    ppermute x4, starting transfers between devices, passed_along(): lax.ppermute(value, axis, [(source, source + steps) for source in range(f...  11.5 us
    all_to_all x1, starting transfers between devices, local(): lax.all_to_all(output_half.reshape(tokens, heads_dev * HD), 'tp', split_a...  6.41 us
    all_to_all x1, starting transfers between devices, local(): lax.all_to_all(pieces, 'tp', split_axis=1, concat_axis=2, tiled=True)  4.24 us
    all_to_all x1, waiting for transfers between devices, local(): lax.all_to_all(output_half.reshape(tokens, heads_dev * HD), 'tp', split_a...  4.22 us
    all_to_all x1, starting transfers between devices, local(): lax.all_to_all(grad_rows, 'tp', split_axis=1, concat_axis=0, tiled=True)  4.11 us
    unnamed x3, local copies, waits for them, and re-layouts  2.93 us
    dot_general x1, matrix products, attend_block(): jnp.einsum('gqtk,kgd->tgqd', d_score, keys_win, preferred_element_type=jn...  2.91 us
  transfers between devices with their start and end apart: 7, of which 6 were waited for; matrix products, arithmetic and copies ran while one was open for 10% of the time, Pallas kernels for 0%

commit v1 on v0

v1 whole, which is shorter than its diff:
```python
import functools
import math

import jax
import jax.numpy as jnp
from jax import lax
from jax.experimental import pallas as pl
from jax.experimental.pallas import tpu as pltpu
from jax.sharding import PartitionSpec as P

H = 32
KVH = 8
HD = 128
BLK = 128
SLOTS = 4
NEG = -1e30
NT = (((1,), (1,)), ((), ()))
F32 = jnp.float32
BF16 = jnp.bfloat16


def kernel(
    dims,
    docs_ref,
    q_ref,
    k_ref,
    v_ref,
    g_ref,
    attn_ref,
    dq_ref,
    dk_ref,
    dv_ref,
    win,
    grads,
    bias,
    outs,
    acc,
    terms,
    arrived,
    fsend,
    final,
    win_send,
    win_recv,
    g_send,
    g_recv,
    o_send,
    o_recv,
    r_send,
    r_recv,
    f_send,
    f_recv,
):
    ctx, tp, groups, per, sharing = dims
    tokens = q_ref.shape[0]
    rows = g_ref.shape[0]
    width = groups * per * HD
    gw = per * HD
    scaling = 1.0 / math.sqrt(HD)
    p = lax.axis_index("ctx")
    t = lax.axis_index("tp")
    even = lax.rem(p, 2) == 0
    odd = jnp.logical_not(even)
    mate = jnp.where(even, p + 1, p - 1)
    low2 = p >= 2
    high2 = p + 2 < ctx
    first_group = t * (groups * per) // (H // KVH)
    my_rows = pl.ds(pl.multiple_of(t * rows, rows), rows)

    def lanes(start, size):
        return pl.ds(pl.multiple_of(start, HD), size)

    barrier = pltpu.get_barrier_semaphore()

    def greet(device):
        pl.semaphore_signal(barrier, inc=1, device_id=device, device_id_type=pl.DeviceIdType.MESH)

    for k in range(1, tp):
        greet({"tp": lax.rem(t + k, tp)})
    greet({"ctx": mate})
    pl.when(low2)(lambda: greet({"ctx": p - 2}))
    pl.when(high2)(lambda: greet({"ctx": p + 2}))
    for j in range(groups):
        cols = lanes((first_group + j) * HD, HD)
        win[j, 0, 0] = k_ref[:, cols]
        win[j, 0, 1] = v_ref[:, cols]
    pl.semaphore_wait(barrier, tp + jnp.where(low2, 1, 0) + jnp.where(high2, 1, 0))

    def remote(src, dst, send, recv, device):
        return pltpu.make_async_remote_copy(
            src_ref=src,
            dst_ref=dst,
            send_sem=send,
            recv_sem=recv,
            device_id=device,
            device_id_type=pl.DeviceIdType.MESH,
        )

    def slab(j, kind, source, slot, device):
        return remote(
            win.at[j, source], win.at[j, slot], win_send.at[j, kind], win_recv.at[j, slot], device
        )

    def grad_copy(j, k):
        peer = lax.rem(t + k, tp)
        return remote(
            g_ref.at[:, lanes(peer * width + j * gw, gw)],
            grads.at[my_rows, pl.ds(j * gw, gw)],
            g_send.at[j, k],
            g_recv.at[j, k],
            {"tp": peer},
        )

    for j in range(groups):
        pl.when(high2)(lambda: slab(j, 0, 0, 2, {"ctx": p + 2}).start())
        pl.when(even)(lambda: slab(j, 1, 0, 1, {"ctx": p + 1}).start())
        for k in range(1, tp):
            grad_copy(j, k).start()

    for d in range(1, SLOTS):

        @pl.when(p < d)
        def _(d=d):
            for j in range(groups):
                win[j, d] = jnp.zeros(win.shape[2:], BF16)

    grads[my_rows, :] = g_ref[:, lanes(t * width, width)]

    for j in range(groups):

        @pl.when(low2)
        def _(j=j):
            slab(j, 0, 0, 2, {"ctx": p - 2}).wait_recv()
            pl.when(even)(lambda: slab(j, 2, 2, 3, {"ctx": p + 1}).start())
            pl.when(odd)(lambda: slab(j, 2, 2, 1, {"ctx": p - 1}).start())

    blocks = tokens // BLK
    ends = []
    total = jnp.int32(0)
    for i in range(docs_ref.shape[0]):
        total = total + docs_ref[i]
        ends.append(total)

    def doc_of(block):
        count = jnp.int32(0)
        for end in ends:
            count = count + jnp.where(end <= block, 1, 0)
        return jnp.where(block >= 0, count, -1)

    causal = lax.broadcasted_iota(jnp.int32, (BLK, BLK), 0) <= lax.broadcasted_iota(
        jnp.int32, (BLK, BLK), 1
    )
    query_docs = [doc_of(p * blocks + b) for b in range(blocks)]
    for d in range(SLOTS):
        for kb in range(blocks):
            key_doc = query_docs[kb] if d == 0 else doc_of((p - d) * blocks + kb)
            for qb in range(blocks):
                if d == 0 and kb > qb:
                    tile = jnp.full((BLK, BLK), NEG, F32)
                elif d == 0 and kb == qb:
                    tile = jnp.where(causal, 0.0, NEG).astype(F32)
                else:
                    level = jnp.where(key_doc == query_docs[qb], 0.0, NEG).astype(F32)
                    tile = jnp.full((BLK, BLK), level, F32)
                bias[pl.ds(d * tokens + kb * BLK, BLK), pl.ds(qb * BLK, BLK)] = tile

    for j in range(groups):
        pl.when(p >= 1)(lambda: slab(j, 0, 0, 1, {"ctx": mate}).wait_recv())
        pl.when(even & low2 & high2)(lambda: slab(j, 3, 1, 3, {"ctx": p + 2}).start())

    span = SLOTS * tokens

    def head(j, i, keys, vals, keys_t, vals_t):
        cols = lanes((j * per + i) * HD, HD)
        queries = q_ref[:, cols]
        grad = grads[:, cols]
        scores = lax.dot_general(keys, queries, NT, preferred_element_type=F32)
        scores = scores * scaling + bias[...]
        e = jnp.exp(scores - jnp.max(scores, axis=0, keepdims=True))
        prob = e * (1.0 / jnp.sum(e, axis=0, keepdims=True))
        half = prob.astype(BF16)
        out_t = jnp.dot(vals_t, half, preferred_element_type=F32).astype(BF16).astype(F32)
        outs[:, cols] = out_t.T.astype(BF16)
        delta = jnp.sum(grad.astype(F32).T * out_t, axis=0, keepdims=True)
        d_prob = lax.dot_general(vals, grad, NT, preferred_element_type=F32)
        d_score = (prob * (d_prob - delta)).astype(BF16)
        dq_t = jnp.dot(keys_t, d_score, preferred_element_type=F32) * scaling
        dq_ref[:, cols] = dq_t.T.astype(BF16)
        d_key = jnp.dot(d_score, queries, preferred_element_type=F32) * scaling
        d_val = jnp.dot(half, grad, preferred_element_type=F32)
        acc[j, :, 0] += d_key.reshape(SLOTS, tokens, HD)
        acc[j, :, 1] += d_val.reshape(SLOTS, tokens, HD)

    def term(j, kind, place, device):
        return remote(
            terms.at[j, kind], arrived.at[j, place], r_send.at[j, kind], r_recv.at[j, place], device
        )

    def out_copy(j, k):
        peer = lax.rem(t + k, tp)
        return remote(
            outs.at[pl.ds(pl.multiple_of(peer * rows, rows), rows), pl.ds(j * gw, gw)],
            attn_ref.at[:, lanes(t * width + j * gw, gw)],
            o_send.at[j, k],
            o_recv.at[j, k],
            {"tp": peer},
        )

    def fin_copy(j, k):
        peer = lax.rem(t + k, tp)
        return remote(
            fsend.at[j, :, pl.ds(pl.multiple_of(peer * rows, rows), rows)],
            final.at[t, j],
            f_send.at[j, k],
            f_recv.at[j, k],
            {"tp": peer},
        )

    def step_a(j):
        @pl.when(p >= 3)
        def _():
            terms[j, 3] = acc[j, 3].astype(BF16)
            pl.when(even)(lambda: term(j, 3, 0, {"ctx": p - 2}).start())
            pl.when(odd)(lambda: term(j, 3, 1, {"ctx": p - 1}).start())

        @pl.when(odd)
        def _():
            terms[j, 1] = acc[j, 1].astype(BF16)
            term(j, 1, 2, {"ctx": p - 1}).start()

    def step_b(j):
        @pl.when(even & low2)
        def _():
            @pl.when(high2)
            def _():
                term(j, 3, 0, {"ctx": p + 2}).wait_recv()
                acc[j, 1] += arrived[j, 0].astype(F32)

            terms[j, 1] = acc[j, 1].astype(BF16)
            term(j, 1, 1, {"ctx": p + 1}).start()

    def step_c(j):
        @pl.when(low2)
        def _():
            term(j, 3, 1, {"ctx": mate}).wait_recv()
            terms[j, 2] = (acc[j, 2] + arrived[j, 1].astype(F32)).astype(BF16)
            term(j, 2, 3, {"ctx": p - 2}).start()

    def step_d(j):
        @pl.when(even)
        def _():
            term(j, 1, 2, {"ctx": p + 1}).wait_recv()
            acc[j, 0] += arrived[j, 2].astype(F32)

        @pl.when(high2)
        def _():
            term(j, 2, 3, {"ctx": p + 2}).wait_recv()
            acc[j, 0] += arrived[j, 3].astype(F32)

        fsend[j] = acc[j, 0].astype(fsend.dtype)
        for k in range(1, tp):
            fin_copy(j, k).start()
        final[t, j] = fsend[j, :, my_rows]

    acc[...] = jnp.zeros(acc.shape, F32)
    pending = []
    for j in range(groups):
        for k in range(1, tp):
            grad_copy(j, k).wait_recv()
        pl.when(low2 & (p >= 3))(lambda: slab(j, 2, 2, 3, {"ctx": mate}).wait_recv())
        keys = win[j, :, 0].reshape(span, HD)
        vals = win[j, :, 1].reshape(span, HD)
        keys_t = keys.astype(F32).T.astype(BF16)
        vals_t = vals.astype(F32).T.astype(BF16)
        if j == 0 and groups > 1:

            @pl.loop(0, per)
            def _(i):
                head(j, i, keys, vals, keys_t, vals_t)
        else:
            for i in range(per):
                head(j, i, keys, vals, keys_t, vals_t)
                if pending:
                    pending.pop(0)()
        for step in pending:
            step()
        step_a(j)
        pending = [functools.partial(f, j) for f in (step_b, step_c, step_d)]
        for k in range(1, tp):
            out_copy(j, k).start()
        cols = lanes(t * width + j * gw, gw)
        attn_ref[:, cols] = outs[my_rows, pl.ds(j * gw, gw)]
    for step in pending:
        step()

    for j in range(groups):
        for k in range(1, tp):
            fin_copy(j, k).wait_recv()
            out_copy(j, k).wait_recv()
    for head_group in range(KVH):
        owner, j = head_group * sharing // groups, head_group % groups
        both = final[owner, j].astype(F32)
        for s in range(1, sharing):
            both = both + final[owner + s, j].astype(F32)
        cols = pl.ds(head_group * HD, HD)
        dk_ref[:, cols] = both[0].astype(BF16)
        dv_ref[:, cols] = both[1].astype(BF16)

    for j in range(groups):
        for k in range(1, tp):
            grad_copy(j, k).wait_send()
            out_copy(j, k).wait_send()
            fin_copy(j, k).wait_send()
        pl.when(high2)(lambda: slab(j, 0, 0, 2, {"ctx": p + 2}).wait_send())
        pl.when(even)(lambda: slab(j, 1, 0, 1, {"ctx": p + 1}).wait_send())
        pl.when(low2)(lambda: slab(j, 2, 2, 3, {"ctx": mate}).wait_send())
        pl.when(even & low2 & high2)(lambda: slab(j, 3, 1, 3, {"ctx": p + 2}).wait_send())
        pl.when(p >= 3)(lambda: term(j, 3, 0, {"ctx": mate}).wait_send())
        pl.when(p >= 1)(lambda: term(j, 1, 2, {"ctx": mate}).wait_send())
        pl.when(low2)(lambda: term(j, 2, 3, {"ctx": p - 2}).wait_send())


def local(ctx, tp, query_heads, key_heads, value_heads, grad_rows, doc_lengths):
    tokens, width = query_heads.shape
    rows = grad_rows.shape[0]
    heads_dev = width // HD
    per_kv = H // KVH
    groups = max(1, heads_dev // per_kv)
    sharing = max(1, per_kv // heads_dev)
    per = heads_dev // groups
    final_type = BF16 if sharing == 1 else F32
    vmem = pl.BlockSpec(memory_space=pltpu.VMEM)
    dma = pltpu.SemaphoreType.DMA
    pair = (2, tokens, HD)
    return pl.pallas_call(
        functools.partial(kernel, (ctx, tp, groups, per, sharing)),
        out_shape=(
            jax.ShapeDtypeStruct((rows, H * HD), BF16),
            jax.ShapeDtypeStruct((tokens, width), BF16),
            jax.ShapeDtypeStruct((rows, KVH * HD), BF16),
            jax.ShapeDtypeStruct((rows, KVH * HD), BF16),
        ),
        in_specs=[pl.BlockSpec(memory_space=pltpu.SMEM)] + [vmem] * 4,
        out_specs=(vmem,) * 4,
        scratch_shapes=[
            pltpu.VMEM((groups, SLOTS) + pair, BF16),
            pltpu.VMEM((tokens, width), BF16),
            pltpu.VMEM((SLOTS * tokens, tokens), F32),
            pltpu.VMEM((tokens, width), BF16),
            pltpu.VMEM((groups, SLOTS) + pair, F32),
            pltpu.VMEM((groups, SLOTS) + pair, BF16),
            pltpu.VMEM((groups, SLOTS) + pair, BF16),
            pltpu.VMEM((groups,) + pair, final_type),
            pltpu.VMEM((tp, groups, 2, rows, HD), final_type),
            dma((groups, 4)),
            dma((groups, SLOTS)),
            dma((groups, tp)),
            dma((groups, tp)),
            dma((groups, tp)),
            dma((groups, tp)),
            dma((groups, SLOTS)),
            dma((groups, SLOTS)),
            dma((groups, tp)),
            dma((groups, tp)),
        ],
        compiler_params=pltpu.CompilerParams(
            collective_id=0, has_side_effects=True, vmem_limit_bytes=48 * 1024 * 1024
        ),
    )(doc_lengths, query_heads, key_heads, value_heads, grad_rows)


def solution(mesh):
    return jax.shard_map(
        functools.partial(local, mesh.shape["ctx"], mesh.shape["tp"]),
        mesh=mesh,
        in_specs=(P("ctx", "tp"), P("ctx", None), P("ctx", None), P(("ctx", "tp"), None), P()),
        out_specs=(
            P(("ctx", "tp"), None),
            P("ctx", "tp"),
            P(("ctx", "tp"), None),
            P(("ctx", "tp"), None),
        ),
        check_vma=False,
    )
```

time: 105 us -> 62.1 us (0.59)
  the two profiles are of different devices: /device:TPU:11 before, /device:TPU:0 now
where the time goes in v1:
time: 62.1 us; the launch traced here: 61.8 us
  Pallas kernels  53.5 us (86%)
  local copies, waits for them, and re-layouts  7.71 us (12%)
  between operations  0.65 us (1%)
    pallas_call x1, Pallas kernels, local(): pl.pallas_call(functools.partial(kernel, (ctx, tp, groups, per, sharing))...  53.5 us
    unnamed x14, local copies, waits for them, and re-layouts  7.71 us

profile of v1, /device:TPU:0, one launch (start us, length us, event | category | flops | bytes accessed | tf_op | source)
XLA Modules:
  0.0 61.8 jit_solution(3728621016489725611)
XLA Ops:
  0.6 0.0 copy-start
  0.6 1.0 %copy-done = bf16[256,1024]{1,0:T(8,128)(2,1)S(1)} copy-done((bf16[256,1024]{1,0:T(8,128)(2,1)S(1)}, bf16[256,1024]{1,0:T(8,128)(2,1)}, u32[]{:S(2)}) %copy-start) | copy-done | bytes 524312
  1.7 0.0 copy-start.1
  1.7 1.0 %copy-done.1 = bf16[256,1024]{1,0:T(8,128)(2,1)S(1)} copy-done((bf16[256,1024]{1,0:T(8,128)(2,1)S(1)}, bf16[256,1024]{1,0:T(8,128)(2,1)}, u32[]{:S(2)}) %copy-start.1) | copy-done | bytes 524312
  2.7 0.0 copy-start.2
  2.7 1.0 %copy-done.2 = bf16[256,1024]{1,0:T(8,128)(2,1)S(1)} copy-done((bf16[256,1024]{1,0:T(8,128)(2,1)S(1)}, bf16[256,1024]{1,0:T(8,128)(2,1)}, u32[]{:S(2)}) %copy-start.2) | copy-done | bytes 524312
  3.8 0.0 copy-start.3
  3.8 1.0 %copy-done.3 = bf16[64,4096]{1,0:T(8,128)(2,1)S(1)} copy-done((bf16[64,4096]{1,0:T(8,128)(2,1)S(1)}, bf16[64,4096]{1,0:T(8,128)(2,1)}, u32[]{:S(2)}) %copy-start.3) | copy-done | bytes 524312
  4.8 0.0 copy-start.4
  4.8 0.7 %copy-done.4 = s32[4]{0:T(128)S(1)} copy-done((s32[4]{0:T(128)S(1)}, s32[4]{0:T(128)}, u32[]{:S(2)}) %copy-start.4) | copy-done | bytes 40
  5.5 53.5 %shard_map.84 = (bf16[64,4096]{1,0:T(8,128)(2,1)S(1)}, bf16[256,1024]{1,0:T(8,128)(2,1)S(1)}, bf16[64,1024]{1,0:T(8,128)(2,1)S(1)}, bf16[64,1024]{1,0:T(8,128)(2,1)S(1)}) custom-call(s32[4]{0:T(128)S(1)} %copy-done.4, bf16[256,1024]{1,0:T(8,128)(2,1)S(1)} %copy-done, bf16[256,1024]{1,0:T(8,128)(2,1)S(1)} %copy-done.1, bf16[256,1024]{1,0:T(8,128)(2,1)S(1)} %copy-done.2, ...), custom_call_target="tpu_custom_call" | custom-call | tf_op jit(solution)/shard_map/pallas_call | solution.py:334
  58.9 0.8 %copy.13 = bf16[64,4096]{1,0:T(8,128)(2,1)} copy(bf16[64,4096]{1,0:T(8,128)(2,1)S(1)} %get-tuple-element.8) | data formatting | bytes 1048576
  59.7 0.8 %copy.14 = bf16[256,1024]{1,0:T(8,128)(2,1)} copy(bf16[256,1024]{1,0:T(8,128)(2,1)S(1)} %get-tuple-element.9) | data formatting | bytes 1048576
  60.5 0.7 %copy.15 = bf16[64,1024]{1,0:T(8,128)(2,1)} copy(bf16[64,1024]{1,0:T(8,128)(2,1)S(1)} %get-tuple-element.10) | data formatting | bytes 262144
  61.2 0.7 %copy.16 = bf16[64,1024]{1,0:T(8,128)(2,1)} copy(bf16[64,1024]{1,0:T(8,128)(2,1)S(1)} %get-tuple-element.11) | data formatting | bytes 262144
Async XLA Ops:
  0.6 1.0 %copy-start = (bf16[256,1024]{1,0:T(8,128)(2,1)S(1)}, bf16[256,1024]{1,0:T(8,128)(2,1)}, u32[]{:S(2)}) copy-start(bf16[256,1024]{1,0:T(8,128)(2,1)} %q_ref.1) | copy-start | bytes 1572868
  1.7 1.0 %copy-start.1 = (bf16[256,1024]{1,0:T(8,128)(2,1)S(1)}, bf16[256,1024]{1,0:T(8,128)(2,1)}, u32[]{:S(2)}) copy-start(bf16[256,1024]{1,0:T(8,128)(2,1)} %k_ref.1) | copy-start | bytes 1572868
  2.7 1.0 %copy-start.2 = (bf16[256,1024]{1,0:T(8,128)(2,1)S(1)}, bf16[256,1024]{1,0:T(8,128)(2,1)}, u32[]{:S(2)}) copy-start(bf16[256,1024]{1,0:T(8,128)(2,1)} %v_ref.1) | copy-start | bytes 1572868
  3.8 1.0 %copy-start.3 = (bf16[64,4096]{1,0:T(8,128)(2,1)S(1)}, bf16[64,4096]{1,0:T(8,128)(2,1)}, u32[]{:S(2)}) copy-start(bf16[64,4096]{1,0:T(8,128)(2,1)} %g_ref.1) | copy-start | bytes 1572868
  4.8 0.7 %copy-start.4 = (s32[4]{0:T(128)S(1)}, s32[4]{0:T(128)}, u32[]{:S(2)}) copy-start(s32[4]{0:T(128)} %docs_ref.1) | copy-start | bytes 52

commit v2 on v1

--- a/solution.py
+++ b/solution.py
@@ -32,7 +32,11 @@
     dv_ref,
     win,
     grads,
+    q_all,
+    g_all,
     bias,
+    probs,
+    dq_sum,
     outs,
     acc,
     terms,
@@ -49,6 +53,7 @@
     r_recv,
     f_send,
     f_recv,
+    in_sem,
 ):
     ctx, tp, groups, per, sharing = dims
     tokens = q_ref.shape[0]
@@ -79,10 +84,26 @@
     greet({"ctx": mate})
     pl.when(low2)(lambda: greet({"ctx": p - 2}))
     pl.when(high2)(lambda: greet({"ctx": p + 2}))
+    loads = []
+
+    def load(src, dst):
+        copy = pltpu.make_async_copy(src, dst, in_sem.at[len(loads)])
+        copy.start()
+        loads.append(copy)
+
     for j in range(groups):
         cols = lanes((first_group + j) * HD, HD)
-        win[j, 0, 0] = k_ref[:, cols]
-        win[j, 0, 1] = v_ref[:, cols]
+        load(k_ref.at[:, cols], win.at[j, 0, 0])
+        load(v_ref.at[:, cols], win.at[j, 0, 1])
+    load(g_ref.at[:, lanes(t * width, width)], grads.at[my_rows])
+    for j in range(groups):
+        for i in range(per):
+            load(
+                q_ref.at[:, pl.ds((j * per + i) * HD, HD)],
+                q_all.at[j, pl.ds(i * tokens, tokens)],
+            )
+    for copy in loads[: 2 * groups]:
+        copy.wait()
     pl.semaphore_wait(barrier, tp + jnp.where(low2, 1, 0) + jnp.where(high2, 1, 0))
 
     def remote(src, dst, send, recv, device):
@@ -122,16 +143,6 @@
         def _(d=d):
             for j in range(groups):
                 win[j, d] = jnp.zeros(win.shape[2:], BF16)
-
-    grads[my_rows, :] = g_ref[:, lanes(t * width, width)]
-
-    for j in range(groups):
-
-        @pl.when(low2)
-        def _(j=j):
-            slab(j, 0, 0, 2, {"ctx": p - 2}).wait_recv()
-            pl.when(even)(lambda: slab(j, 2, 2, 3, {"ctx": p + 1}).start())
-            pl.when(odd)(lambda: slab(j, 2, 2, 1, {"ctx": p - 1}).start())
 
     blocks = tokens // BLK
     ends = []
@@ -163,32 +174,80 @@
                     tile = jnp.full((BLK, BLK), level, F32)
                 bias[pl.ds(d * tokens + kb * BLK, BLK), pl.ds(qb * BLK, BLK)] = tile
 
+    for copy in loads[2 * groups :]:
+        copy.wait()
+
+    def scores(j, d):
+        wide = lax.dot_general(win[j, d, 0], q_all[j], NT, preferred_element_type=F32)
+        tile = bias[pl.ds(d * tokens, tokens), :]
+        probs[j, d] = wide * scaling + jnp.concatenate([tile] * per, axis=1)
+
+    for j in range(groups):
+
+        @pl.when(low2)
+        def _(j=j):
+            slab(j, 0, 0, 2, {"ctx": p - 2}).wait_recv()
+            pl.when(even)(lambda: slab(j, 2, 2, 3, {"ctx": p + 1}).start())
+            pl.when(odd)(lambda: slab(j, 2, 2, 1, {"ctx": p - 1}).start())
+
+    for j in range(groups):
+        scores(j, 0)
     for j in range(groups):
         pl.when(p >= 1)(lambda: slab(j, 0, 0, 1, {"ctx": mate}).wait_recv())
         pl.when(even & low2 & high2)(lambda: slab(j, 3, 1, 3, {"ctx": p + 2}).start())
 
-    span = SLOTS * tokens
-
-    def head(j, i, keys, vals, keys_t, vals_t):
-        cols = lanes((j * per + i) * HD, HD)
-        queries = q_ref[:, cols]
-        grad = grads[:, cols]
-        scores = lax.dot_general(keys, queries, NT, preferred_element_type=F32)
-        scores = scores * scaling + bias[...]
-        e = jnp.exp(scores - jnp.max(scores, axis=0, keepdims=True))
-        prob = e * (1.0 / jnp.sum(e, axis=0, keepdims=True))
-        half = prob.astype(BF16)
-        out_t = jnp.dot(vals_t, half, preferred_element_type=F32).astype(BF16).astype(F32)
-        outs[:, cols] = out_t.T.astype(BF16)
-        delta = jnp.sum(grad.astype(F32).T * out_t, axis=0, keepdims=True)
-        d_prob = lax.dot_general(vals, grad, NT, preferred_element_type=F32)
+    for j in range(groups):
+        scores(j, 2)
+    for j in range(groups):
+        scores(j, 1)
+
+    def across(value):
+        return value.astype(F32).T
+
+    def forward(j):
+        top = jnp.max(probs[j, 0], axis=0, keepdims=True)
+        for d in range(1, SLOTS):
+            top = jnp.maximum(top, jnp.max(probs[j, d], axis=0, keepdims=True))
+        norm = jnp.zeros_like(top)
+        for d in range(SLOTS):
+            e = jnp.exp(probs[j, d] - top)
+            probs[j, d] = e
+            norm = norm + jnp.sum(e, axis=0, keepdims=True)
+        inverse = 1.0 / norm
+        out_t = jnp.zeros((HD, per * tokens), F32)
+        for d in range(SLOTS):
+            prob = probs[j, d] * inverse
+            probs[j, d] = prob
+            vals_t = across(win[j, d, 1]).astype(BF16)
+            out_t = out_t + jnp.dot(vals_t, prob.astype(BF16), preferred_element_type=F32)
+        out_t = out_t.astype(BF16).astype(F32)
+        rows_of = out_t.T.astype(BF16)
+        for i in range(per):
+            cols = pl.ds((j * per + i) * HD, HD)
+            outs[:, cols] = rows_of[i * tokens : (i + 1) * tokens]
+        return out_t
+
+    def delta_of(j, out_t):
+        for i in range(per):
+            cols = pl.ds((j * per + i) * HD, HD)
+            g_all[j, pl.ds(i * tokens, tokens)] = grads[:, cols]
+        return jnp.sum(across(g_all[j]) * out_t, axis=0, keepdims=True)
+
+    def backward(j, d, delta, first):
+        d_prob = lax.dot_general(win[j, d, 1], g_all[j], NT, preferred_element_type=F32)
+        prob = probs[j, d]
         d_score = (prob * (d_prob - delta)).astype(BF16)
-        dq_t = jnp.dot(keys_t, d_score, preferred_element_type=F32) * scaling
-        dq_ref[:, cols] = dq_t.T.astype(BF16)
-        d_key = jnp.dot(d_score, queries, preferred_element_type=F32) * scaling
-        d_val = jnp.dot(half, grad, preferred_element_type=F32)
-        acc[j, :, 0] += d_key.reshape(SLOTS, tokens, HD)
-        acc[j, :, 1] += d_val.reshape(SLOTS, tokens, HD)
+        keys_t = across(win[j, d, 0]).astype(BF16)
+        dq_t = jnp.dot(keys_t, d_score, preferred_element_type=F32)
+        dq_sum[j] = dq_t if first else dq_sum[j] + dq_t
+        acc[j, d, 0] = jnp.dot(d_score, q_all[j], preferred_element_type=F32) * scaling
+        acc[j, d, 1] = jnp.dot(prob.astype(BF16), g_all[j], preferred_element_type=F32)
+
+    def finish_query(j):
+        rows_of = (dq_sum[j] * scaling).T.astype(BF16)
+        for i in range(per):
+            cols = pl.ds((j * per + i) * HD, HD)
+            dq_ref[:, cols] = rows_of[i * tokens : (i + 1) * tokens]
 
     def term(j, kind, place, device):
         return remote(
@@ -215,13 +274,14 @@
             {"tp": peer},
         )
 
-    def step_a(j):
+    def step_a3(j):
         @pl.when(p >= 3)
         def _():
             terms[j, 3] = acc[j, 3].astype(BF16)
             pl.when(even)(lambda: term(j, 3, 0, {"ctx": p - 2}).start())
             pl.when(odd)(lambda: term(j, 3, 1, {"ctx": p - 1}).start())
 
+    def step_a1(j):
         @pl.when(odd)
         def _():
             terms[j, 1] = acc[j, 1].astype(BF16)
@@ -261,36 +321,34 @@
             fin_copy(j, k).start()
         final[t, j] = fsend[j, :, my_rows]
 
-    acc[...] = jnp.zeros(acc.shape, F32)
-    pending = []
-    for j in range(groups):
-        for k in range(1, tp):
-            grad_copy(j, k).wait_recv()
-        pl.when(low2 & (p >= 3))(lambda: slab(j, 2, 2, 3, {"ctx": mate}).wait_recv())
-        keys = win[j, :, 0].reshape(span, HD)
-        vals = win[j, :, 1].reshape(span, HD)
-        keys_t = keys.astype(F32).T.astype(BF16)
-        vals_t = vals.astype(F32).T.astype(BF16)
-        if j == 0 and groups > 1:
-
-            @pl.loop(0, per)
-            def _(i):
-                head(j, i, keys, vals, keys_t, vals_t)
-        else:
-            for i in range(per):
-                head(j, i, keys, vals, keys_t, vals_t)
-                if pending:
-                    pending.pop(0)()
-        for step in pending:
-            step()
-        step_a(j)
-        pending = [functools.partial(f, j) for f in (step_b, step_c, step_d)]
+    deltas = []
+    for j in range(groups):
+        pl.when(p >= 3)(lambda: slab(j, 2, 2, 3, {"ctx": mate}).wait_recv())
+        scores(j, 3)
+        out_t = forward(j)
         for k in range(1, tp):
             out_copy(j, k).start()
         cols = lanes(t * width + j * gw, gw)
         attn_ref[:, cols] = outs[my_rows, pl.ds(j * gw, gw)]
-    for step in pending:
-        step()
+        for k in range(1, tp):
+            grad_copy(j, k).wait_recv()
+        deltas.append(delta_of(j, out_t))
+    for j in range(groups):
+        backward(j, 3, deltas[j], True)
+        step_a3(j)
+    for j in range(groups):
+        backward(j, 1, deltas[j], False)
+        step_a1(j)
+    for j in range(groups):
+        step_b(j)
+        backward(j, 2, deltas[j], False)
+    for j in range(groups):
+        backward(j, 0, deltas[j], False)
+        step_c(j)
+    for j in range(groups):
+        finish_query(j)
+    for j in range(groups):
+        step_d(j)
 
     for j in range(groups):
         for k in range(1, tp):
@@ -339,12 +397,16 @@
             jax.ShapeDtypeStruct((rows, KVH * HD), BF16),
             jax.ShapeDtypeStruct((rows, KVH * HD), BF16),
         ),
-        in_specs=[pl.BlockSpec(memory_space=pltpu.SMEM)] + [vmem] * 4,
+        in_specs=[pl.BlockSpec(memory_space=pltpu.SMEM)] + [pl.BlockSpec(memory_space=pltpu.HBM)] * 4,
         out_specs=(vmem,) * 4,
         scratch_shapes=[
             pltpu.VMEM((groups, SLOTS) + pair, BF16),
             pltpu.VMEM((tokens, width), BF16),
+            pltpu.VMEM((groups, per * tokens, HD), BF16),
+            pltpu.VMEM((groups, per * tokens, HD), BF16),
             pltpu.VMEM((SLOTS * tokens, tokens), F32),
+            pltpu.VMEM((groups, SLOTS, tokens, per * tokens), F32),
+            pltpu.VMEM((groups, HD, per * tokens), F32),
             pltpu.VMEM((tokens, width), BF16),
             pltpu.VMEM((groups, SLOTS) + pair, F32),
             pltpu.VMEM((groups, SLOTS) + pair, BF16),
@@ -361,9 +423,10 @@
             dma((groups, SLOTS)),
             dma((groups, tp)),
             dma((groups, tp)),
+            dma((2 * groups + 1 + groups * per,)),
         ],
         compiler_params=pltpu.CompilerParams(
-            collective_id=0, has_side_effects=True, vmem_limit_bytes=48 * 1024 * 1024
+            collective_id=0, has_side_effects=True, vmem_limit_bytes=62 * 1024 * 1024
         ),
     )(doc_lengths, query_heads, key_heads, value_heads, grad_rows)
 

time: 62.1 us -> 48.9 us (0.79)
  the two profiles are of different devices: /device:TPU:0 before, /device:TPU:11 now
where the time goes in v2:
time: 48.9 us; the launch traced here: 48.7 us
  Pallas kernels  43.5 us (89%)
  local copies, waits for them, and re-layouts  4.56 us (9%)
  between operations  0.65 us (1%)
    pallas_call x1, Pallas kernels, local(): pl.pallas_call(functools.partial(kernel, (ctx, tp, groups, per, sharing))...  43.5 us
    unnamed x10, local copies, waits for them, and re-layouts  4.56 us

profile of v2, /device:TPU:11, one launch (start us, length us, event | category | flops | bytes accessed | tf_op | source)
XLA Modules:
  0.0 48.7 jit_solution(1018281046969615965)
XLA Ops:
  0.6 43.5 %shard_map.84 = (bf16[64,4096]{1,0:T(8,128)(2,1)}, bf16[256,1024]{1,0:T(8,128)(2,1)}, bf16[64,1024]{1,0:T(8,128)(2,1)}, bf16[64,1024]{1,0:T(8,128)(2,1)}) custom-call(s32[4]{0:T(128)} %docs_ref.1, bf16[256,1024]{1,0:T(8,128)(2,1)} %q_ref.1, bf16[256,1024]{1,0:T(8,128)(2,1)} %k_ref.1, bf16[256,1024]{1,0:T(8,128)(2,1)} %v_ref.1, bf16[64,4096]{1,0:T(8,128)(2,1)} %g_ref.1), custom_call_target="tpu_custom_call" | custom-call | tf_op jit(solution)/shard_map/pallas_call | solution.py:392
  44.2 0.0 copy-start
  44.2 1.9 %copy.13 = bf16[64,4096]{1,0:T(8,128)(2,1)} copy(bf16[64,4096]{1,0:T(8,128)(2,1)} %get-tuple-element.8) | data formatting | bytes 1048576
  46.1 0.0 copy-done
  46.1 0.0 copy-start.2
  46.1 0.8 %copy.14 = bf16[256,1024]{1,0:T(8,128)(2,1)} copy(bf16[256,1024]{1,0:T(8,128)(2,1)S(1)} %copy-done) | data formatting | bytes 1048576
  46.9 0.2 copy-done.2
  47.1 0.0 copy-start.1
  47.1 0.7 %copy.15 = bf16[64,1024]{1,0:T(8,128)(2,1)} copy(bf16[64,1024]{1,0:T(8,128)(2,1)S(1)} %copy-done.2) | data formatting | bytes 262144
  47.8 0.3 copy-done.1
  48.1 0.7 %copy.16 = bf16[64,1024]{1,0:T(8,128)(2,1)} copy(bf16[64,1024]{1,0:T(8,128)(2,1)S(1)} %copy-done.1) | data formatting | bytes 262144
Async XLA Ops:
  44.2 1.9 %copy-start = (bf16[256,1024]{1,0:T(8,128)(2,1)S(1)}, bf16[256,1024]{1,0:T(8,128)(2,1)}, u32[]{:S(2)}) copy-start(bf16[256,1024]{1,0:T(8,128)(2,1)} %get-tuple-element.9) | copy-start | bytes 1572868
  46.1 1.0 %copy-start.2 = (bf16[64,1024]{1,0:T(8,128)(2,1)S(1)}, bf16[64,1024]{1,0:T(8,128)(2,1)}, u32[]{:S(2)}) copy-start(bf16[64,1024]{1,0:T(8,128)(2,1)} %get-tuple-element.10) | copy-start | bytes 393220
  47.1 1.0 %copy-start.1 = (bf16[64,1024]{1,0:T(8,128)(2,1)S(1)}, bf16[64,1024]{1,0:T(8,128)(2,1)}, u32[]{:S(2)}) copy-start(bf16[64,1024]{1,0:T(8,128)(2,1)} %get-tuple-element.11) | copy-start | bytes 393220

commit v3 on v2

--- a/solution.py
+++ b/solution.py
@@ -54,6 +54,9 @@
     f_send,
     f_recv,
     in_sem,
+    dq_held,
+    kv_held,
+    out_sem,
 ):
     ctx, tp, groups, per, sharing = dims
     tokens = q_ref.shape[0]
@@ -247,7 +250,9 @@
         rows_of = (dq_sum[j] * scaling).T.astype(BF16)
         for i in range(per):
             cols = pl.ds((j * per + i) * HD, HD)
-            dq_ref[:, cols] = rows_of[i * tokens : (i + 1) * tokens]
+            dq_held[:, cols] = rows_of[i * tokens : (i + 1) * tokens]
+        cols = pl.ds(j * gw, gw)
+        store(dq_held.at[:, cols], dq_ref.at[:, cols])
 
     def term(j, kind, place, device):
         return remote(
@@ -322,6 +327,13 @@
         final[t, j] = fsend[j, :, my_rows]
 
     deltas = []
+    stores = []
+
+    def store(src, dst):
+        copy = pltpu.make_async_copy(src, dst, out_sem.at[len(stores)])
+        copy.start()
+        stores.append(copy)
+
     for j in range(groups):
         pl.when(p >= 3)(lambda: slab(j, 2, 2, 3, {"ctx": mate}).wait_recv())
         scores(j, 3)
@@ -329,7 +341,7 @@
         for k in range(1, tp):
             out_copy(j, k).start()
         cols = lanes(t * width + j * gw, gw)
-        attn_ref[:, cols] = outs[my_rows, pl.ds(j * gw, gw)]
+        store(outs.at[my_rows, pl.ds(j * gw, gw)], attn_ref.at[:, cols])
         for k in range(1, tp):
             grad_copy(j, k).wait_recv()
         deltas.append(delta_of(j, out_t))
@@ -353,20 +365,22 @@
     for j in range(groups):
         for k in range(1, tp):
             fin_copy(j, k).wait_recv()
-            out_copy(j, k).wait_recv()
     for head_group in range(KVH):
         owner, j = head_group * sharing // groups, head_group % groups
         both = final[owner, j].astype(F32)
         for s in range(1, sharing):
             both = both + final[owner + s, j].astype(F32)
         cols = pl.ds(head_group * HD, HD)
-        dk_ref[:, cols] = both[0].astype(BF16)
-        dv_ref[:, cols] = both[1].astype(BF16)
+        kv_held[0, :, cols] = both[0].astype(BF16)
+        kv_held[1, :, cols] = both[1].astype(BF16)
+    store(kv_held.at[0], dk_ref)
+    store(kv_held.at[1], dv_ref)
 
     for j in range(groups):
         for k in range(1, tp):
             grad_copy(j, k).wait_send()
             out_copy(j, k).wait_send()
+            out_copy(j, k).wait_recv()
             fin_copy(j, k).wait_send()
         pl.when(high2)(lambda: slab(j, 0, 0, 2, {"ctx": p + 2}).wait_send())
         pl.when(even)(lambda: slab(j, 1, 0, 1, {"ctx": p + 1}).wait_send())
@@ -375,6 +389,17 @@
         pl.when(p >= 3)(lambda: term(j, 3, 0, {"ctx": mate}).wait_send())
         pl.when(p >= 1)(lambda: term(j, 1, 2, {"ctx": mate}).wait_send())
         pl.when(low2)(lambda: term(j, 2, 3, {"ctx": p - 2}).wait_send())
+    for copy in stores:
+        copy.wait()
+
+
+def write_out(*refs):
+    sources, targets, sems = refs[:4], refs[4:8], refs[8]
+    copies = [pltpu.make_async_copy(sources[i], targets[i], sems.at[i]) for i in range(4)]
+    for copy in copies:
+        copy.start()
+    for copy in copies:
+        copy.wait()
 
 
 def local(ctx, tp, query_heads, key_heads, value_heads, grad_rows, doc_lengths):
@@ -386,10 +411,11 @@
     sharing = max(1, per_kv // heads_dev)
     per = heads_dev // groups
     final_type = BF16 if sharing == 1 else F32
-    vmem = pl.BlockSpec(memory_space=pltpu.VMEM)
+    hbm = pl.BlockSpec(memory_space=pltpu.HBM)
+    limit = 62 * 1024 * 1024
     dma = pltpu.SemaphoreType.DMA
     pair = (2, tokens, HD)
-    return pl.pallas_call(
+    results = pl.pallas_call(
         functools.partial(kernel, (ctx, tp, groups, per, sharing)),
         out_shape=(
             jax.ShapeDtypeStruct((rows, H * HD), BF16),
@@ -397,8 +423,8 @@
             jax.ShapeDtypeStruct((rows, KVH * HD), BF16),
             jax.ShapeDtypeStruct((rows, KVH * HD), BF16),
         ),
-        in_specs=[pl.BlockSpec(memory_space=pltpu.SMEM)] + [pl.BlockSpec(memory_space=pltpu.HBM)] * 4,
-        out_specs=(vmem,) * 4,
+        in_specs=[pl.BlockSpec(memory_space=pltpu.SMEM)] + [hbm] * 4,
+        out_specs=(hbm,) * 4,
         scratch_shapes=[
             pltpu.VMEM((groups, SLOTS) + pair, BF16),
             pltpu.VMEM((tokens, width), BF16),
@@ -424,11 +450,22 @@
             dma((groups, tp)),
             dma((groups, tp)),
             dma((2 * groups + 1 + groups * per,)),
+            pltpu.VMEM((tokens, width), BF16),
+            pltpu.VMEM((2, rows, KVH * HD), BF16),
+            dma((2 * groups + 2,)),
         ],
         compiler_params=pltpu.CompilerParams(
-            collective_id=0, has_side_effects=True, vmem_limit_bytes=62 * 1024 * 1024
+            collective_id=0, has_side_effects=True, vmem_limit_bytes=limit
         ),
     )(doc_lengths, query_heads, key_heads, value_heads, grad_rows)
+    return pl.pallas_call(
+        write_out,
+        out_shape=tuple(jax.ShapeDtypeStruct(r.shape, r.dtype) for r in results),
+        in_specs=[hbm] * 4,
+        out_specs=(hbm,) * 4,
+        scratch_shapes=[dma((4,))],
+        compiler_params=pltpu.CompilerParams(vmem_limit_bytes=limit),
+    )(*results)
 
 
 def solution(mesh):

time: 48.9 us -> 84.8 us (1.73)
  Pallas kernels: 43.5 us -> 84 us
  local copies, waits for them, and re-layouts: 4.56 us -> 0 us
    pallas_call x0 -> x1, Pallas kernels: none -> 40.8 us  [local(): pl.pallas_call(write_out, out_shape=tuple((jax.ShapeDtypeStruct(r.shape,...]
    unnamed x10 -> x0, local copies, waits for them, and re-layouts: 4.56 us -> none
where the time goes in v3:
time: 84.8 us; the launch traced here: 84.7 us
  Pallas kernels  84 us (99%)
    pallas_call x1, Pallas kernels, local(): pl.pallas_call(functools.partial(kernel, (ctx, tp, groups, per, sharing))...  43.2 us
    pallas_call x1, Pallas kernels, local(): pl.pallas_call(write_out, out_shape=tuple((jax.ShapeDtypeStruct(r.shape,...  40.8 us

profile of v3, /device:TPU:11, one launch (start us, length us, event | category | flops | bytes accessed | tf_op | source)
XLA Modules:
  0.0 84.7 jit_solution(16353515374478997049)
XLA Ops:
  0.6 43.2 %shard_map.84 = (bf16[64,4096]{1,0:T(8,128)(2,1)}, bf16[256,1024]{1,0:T(8,128)(2,1)}, bf16[64,1024]{1,0:T(8,128)(2,1)}, bf16[64,1024]{1,0:T(8,128)(2,1)}) custom-call(s32[4]{0:T(128)} %docs_ref.1, bf16[256,1024]{1,0:T(8,128)(2,1)} %q_ref.1, bf16[256,1024]{1,0:T(8,128)(2,1)} %k_ref.1, bf16[256,1024]{1,0:T(8,128)(2,1)} %v_ref.1, bf16[64,4096]{1,0:T(8,128)(2,1)} %g_ref.1), custom_call_target="tpu_custom_call" | custom-call | tf_op jit(solution)/shard_map/pallas_call | solution.py:418
  43.8 40.8 %shard_map.85 = (bf16[64,4096]{1,0:T(8,128)(2,1)}, bf16[256,1024]{1,0:T(8,128)(2,1)}, bf16[64,1024]{1,0:T(8,128)(2,1)}, bf16[64,1024]{1,0:T(8,128)(2,1)}) custom-call(bf16[64,4096]{1,0:T(8,128)(2,1)} %get-tuple-element.8.refs_0_, bf16[256,1024]{1,0:T(8,128)(2,1)} %get-tuple-element.9.refs_1_, bf16[64,1024]{1,0:T(8,128)(2,1)} %get-tuple-element.10.refs_2_, ...), custom_call_target="tpu_custom_call" | custom-call | tf_op jit(solution)/shard_map/pallas_call | solution.py:461

commit v4 on v3

--- a/solution.py
+++ b/solution.py
@@ -394,11 +394,15 @@
 
 
 def write_out(*refs):
-    sources, targets, sems = refs[:4], refs[4:8], refs[8]
-    copies = [pltpu.make_async_copy(sources[i], targets[i], sems.at[i]) for i in range(4)]
-    for copy in copies:
+    sources, targets, held, sems = refs[:4], refs[4:8], refs[8:12], refs[12]
+    reads = [pltpu.make_async_copy(sources[i], held[i], sems.at[0, i]) for i in range(4)]
+    writes = [pltpu.make_async_copy(held[i], targets[i], sems.at[1, i]) for i in range(4)]
+    for copy in reads:
         copy.start()
-    for copy in copies:
+    for read, write in zip(reads, writes):
+        read.wait()
+        write.start()
+    for copy in writes:
         copy.wait()
 
 
@@ -463,7 +467,7 @@
         out_shape=tuple(jax.ShapeDtypeStruct(r.shape, r.dtype) for r in results),
         in_specs=[hbm] * 4,
         out_specs=(hbm,) * 4,
-        scratch_shapes=[dma((4,))],
+        scratch_shapes=[pltpu.VMEM(r.shape, r.dtype) for r in results] + [dma((2, 4))],
         compiler_params=pltpu.CompilerParams(vmem_limit_bytes=limit),
     )(*results)
 

time: 84.8 us -> 46.1 us (0.54)
  Pallas kernels: 84 us -> 45.3 us
    pallas_call x1, Pallas kernels: 40.8 us -> 2.16 us  [local(): pl.pallas_call(write_out, out_shape=tuple((jax.ShapeDtypeStruct(r.shape,...]
where the time goes in v4:
time: 46.1 us; the launch traced here: 46 us
  Pallas kernels  45.3 us (98%)
  between operations  0.64 us (1%)
    pallas_call x1, Pallas kernels, local(): pl.pallas_call(functools.partial(kernel, (ctx, tp, groups, per, sharing))...  43.2 us
    pallas_call x1, Pallas kernels, local(): pl.pallas_call(write_out, out_shape=tuple((jax.ShapeDtypeStruct(r.shape,...  2.16 us

profile of v4, /device:TPU:11, one launch (start us, length us, event | category | flops | bytes accessed | tf_op | source)
XLA Modules:
  0.0 46.0 jit_solution(4974413988169698478)
XLA Ops:
  0.6 43.2 %shard_map.84 = (bf16[64,4096]{1,0:T(8,128)(2,1)}, bf16[256,1024]{1,0:T(8,128)(2,1)}, bf16[64,1024]{1,0:T(8,128)(2,1)}, bf16[64,1024]{1,0:T(8,128)(2,1)}) custom-call(s32[4]{0:T(128)} %docs_ref.1, bf16[256,1024]{1,0:T(8,128)(2,1)} %q_ref.1, bf16[256,1024]{1,0:T(8,128)(2,1)} %k_ref.1, bf16[256,1024]{1,0:T(8,128)(2,1)} %v_ref.1, bf16[64,4096]{1,0:T(8,128)(2,1)} %g_ref.1), custom_call_target="tpu_custom_call" | custom-call | tf_op jit(solution)/shard_map/pallas_call | solution.py:422
  43.8 2.2 %shard_map.85 = (bf16[64,4096]{1,0:T(8,128)(2,1)}, bf16[256,1024]{1,0:T(8,128)(2,1)}, bf16[64,1024]{1,0:T(8,128)(2,1)}, bf16[64,1024]{1,0:T(8,128)(2,1)}) custom-call(bf16[64,4096]{1,0:T(8,128)(2,1)} %get-tuple-element.8.refs_0_, bf16[256,1024]{1,0:T(8,128)(2,1)} %get-tuple-element.9.refs_1_, bf16[64,1024]{1,0:T(8,128)(2,1)} %get-tuple-element.10.refs_2_, ...), custom_call_target="tpu_custom_call" | custom-call | tf_op jit(solution)/shard_map/pallas_call | solution.py:465
